TPU v7x, 256 devices: a whole 4x4x8 slice. The times are simulated.
256 devices in a mesh: row: 16 (over y, x), col: 16 (over z, core).
Axes of the slice: x: 4, y: 4, z: 8, core: 2. Of those that a mesh axis runs over, the one named last changes fastest.
Arguments:
- points: float32 [3, 32768], P(None, ('row', 'col')), may hold values from -0.03 to 8, as said below
- amplitude: float32 [32768], P(('row', 'col')), may hold values from 0.5 to 2
- sketch: bfloat16 [32768, 512], P(('row', 'col')), may hold values from -6 to 6
Outputs:
- kl_modes: float32 [32768, 512], P(('row', 'col'))
Inputs may be any that keep to these rules, and one draw needn't show every extreme that they name: `points`: each point lies near a lattice site of spacing 1/16, sixteen sites along x and y.
All inputs are finite; a program needn't handle non-finite values.
Results may differ from a plain program's by a relative error of at most 0.0003.
The roundings to bfloat16 on the way count: a program that leaves them out, or rounds other values in their place, can miss the bound.
Values may be sent and summed in bfloat16 or wider, within the bound.
A program may use at most 64 MiB of HBM per device.

v0:
```python
import math

import jax
import jax.numpy as jnp
from jax import lax
from jax.sharding import PartitionSpec as P

NS_ITERS = 3


correlation = 4.0


def kernel_tile(row_pts, row_amp, row_index, col_pts, col_amp, col_index, weight):
    distance = jnp.zeros((row_pts.shape[1], col_pts.shape[1]), jnp.float32)
    for component in range(3):
        offset = row_pts[component][:, None] - col_pts[component][None, :]
        distance = distance + offset * offset
    covariance = (
        weight * row_amp[:, None] * col_amp[None, :] * jnp.exp(-jnp.sqrt(distance) / correlation)
    )
    covariance = covariance + (row_index[:, None] == col_index[None, :]).astype(jnp.float32)
    return covariance.astype(jnp.bfloat16)


def per_device(points, amplitude, sketch):
    highest = lax.Precision.HIGHEST
    local_pts = points.shape[1]
    rank_cols = sketch.shape[1]
    row_count_axis = lax.axis_size("row")
    col_count_axis = lax.axis_size("col")
    weight = 0.5 / math.sqrt(local_pts * row_count_axis * col_count_axis)
    row_place = lax.axis_index("row")
    col_place = lax.axis_index("col")
    span = local_pts * col_count_axis
    block_index = row_place * span + jnp.arange(span, dtype=jnp.int32)
    stripe_pos = jnp.arange(local_pts * row_count_axis, dtype=jnp.int32)
    stripe_index = stripe_pos // local_pts * span + col_place * local_pts + stripe_pos % local_pts
    block_pts, block_amp = (
        lax.all_gather(points, "col", axis=1, tiled=True),
        lax.all_gather(amplitude, "col", axis=0, tiled=True),
    )
    stripe_pts, stripe_amp = (
        lax.all_gather(points, "row", axis=1, tiled=True),
        lax.all_gather(amplitude, "row", axis=0, tiled=True),
    )
    stripe_rows = lax.all_gather(sketch, "row", axis=0, tiled=True)
    kernel_block = kernel_tile(
        block_pts, block_amp, block_index, stripe_pts, stripe_amp, stripe_index, weight
    )
    own_rows = lax.psum_scatter(
        jnp.dot(kernel_block, stripe_rows, preferred_element_type=jnp.float32),
        "col",
        scatter_dimension=0,
        tiled=True,
    )
    gram_matrix = lax.psum(jnp.dot(own_rows.T, own_rows, precision=highest), ("row", "col"))
    norm_gram = jnp.sqrt(jnp.sum(gram_matrix * gram_matrix))
    iterate = gram_matrix / norm_gram
    identity = jnp.eye(rank_cols, dtype=jnp.float32)
    partner = identity
    for newton_step in range(NS_ITERS):
        middle = 1.5 * identity - 0.5 * jnp.dot(partner, iterate, precision=highest)
        iterate, partner = (
            jnp.dot(iterate, middle, precision=highest),
            jnp.dot(middle, partner, precision=highest),
        )
    rotation = partner / jnp.sqrt(norm_gram)
    return math.sqrt(rank_cols) * jnp.dot(own_rows, rotation, precision=highest)


def solution(mesh):
    in_specs = (P(None, ("row", "col")), P(("row", "col")), P(("row", "col"), None))
    out_specs = P(("row", "col"), None)
    return jax.shard_map(
        per_device, mesh=mesh, in_specs=in_specs, out_specs=out_specs, check_vma=False
    )
```

profile of v0, /device:TPU:1, one launch (start us, length us, event | category | flops | bytes accessed | tf_op | source)
XLA Modules:
  0.0 445.4 jit_solution(8547112257782904929)
XLA Ops:
  6.5 0.0 all-gather.4.cloned.1.call-start
  6.5 0.7 all-gather.4.cloned.1.call-update
  7.3 0.0 reduce-scatter.2.cloned.1.call-start
  7.3 17.2 %all-gather.1 = f32[16,1,128]{2,1,0:T(1,128)S(1)} all-gather(f32[1,1,128]{2,1,0:T(1,128)} %bitcast.34), channel_id=1, replica_groups=mesh['row'=16,'col'=16] {'row'}, dimensions={0}, use_global_device_ids=true | all-gather | bytes 8704 | tf_op jit(solution)/shard_map/all_gather | solution.py:45
  24.5 25.0 %all-gather = f32[16,1,128]{2,1,0:T(1,128)S(1)} all-gather(f32[1,1,128]{2,1,0:T(1,128)} %bitcast.35), channel_id=1, replica_groups=mesh['row'=16,'col'=16] {'col'}, dimensions={0}, use_global_device_ids=true | all-gather | bytes 8704 | tf_op jit(solution)/shard_map/all_gather | solution.py:41
  49.5 17.7 %all_gather.18 = f32[3,2048]{1,0:T(4,128)S(1)} all-gather(f32[3,128]{1,0:T(4,128)} %param.3), channel_id=1, replica_groups=mesh['row'=16,'col'=16] {'row'}, dimensions={1}, use_global_device_ids=true | all-gather | bytes 26112 | tf_op jit(solution)/shard_map/all_gather | solution.py:44
  67.3 18.8 %all_gather.17 = f32[3,2048]{1,0:T(4,128)S(1)} all-gather(f32[3,128]{1,0:T(4,128)} %param.3), channel_id=1, replica_groups=mesh['row'=16,'col'=16] {'col'}, dimensions={1}, use_global_device_ids=true | all-gather | bytes 26112 | tf_op jit(solution)/shard_map/all_gather | solution.py:40
  86.2 0.0 all-gather.4.cloned.1.call-done
  86.2 16.1 %fusion = f32[2048,512]{1,0:T(8,128)} fusion(bf16[2048,512]{1,0:T(8,128)(2,1)} %all-gather.4.cloned.1.call-done, s32[2048]{0:T(1024)S(1)} %get-tuple-element.11, f32[2048]{0:T(1024)S(1)} %bitcast.29, f32[2048]{0:T(1024)S(1)} %bitcast.32, f32[2048]{0:T(1024)S(1)} %bitcast.30, f32[2048]{0:T(1024)S(1)} %bitcast.33, f32[2048]{0:T(1024)S(1)} %bitcast.28, ...), kind=kOutput, calls=%fused_computation.1 | convolution fusion | flops 4362076160 | bytes 6373376 | tf_op jit(solution)/shard_map/dot_general | solution.py:52
  102.3 0.0 reduce-scatter.2.cloned.1.call-update
  102.3 0.2 all-reduce.2.cloned.1.call-start
  102.6 55.8 %reduce-scatter.2.cloned.1.call-done = f32[128,512]{1,0:T(8,128)} async-done(((f32[2048,512]{1,0:T(8,128)}), f32[128,512]{1,0:T(8,128)}) %reduce-scatter.2.cloned.1.call-update) | async-done | bytes 262160 | tf_op jit(solution)/shard_map/reduce_scatter | solution.py:51
  158.4 3.1 fusion.27
  161.5 0.0 all-reduce.2.cloned.1.call-update
  161.5 258.3 %all-reduce.2.cloned.1.call-done = f32[512,512]{1,0:T(8,128)} async-done(((f32[512,512]{1,0:T(8,128)}), f32[512,512]{1,0:T(8,128)}) %all-reduce.2.cloned.1.call-update) | async-done | bytes 1048592 | tf_op jit(solution)/shard_map/psum | solution.py:57
  419.8 0.0 copy-start.1
  419.8 2.2 multiply_reduce_fusion
  422.7 2.3 select_subtract_fusion.2
  425.0 1.0 fusion.12
  426.0 0.0 copy-done.1
  426.0 1.9 fusion.13
  427.9 1.9 select_subtract_fusion.1
  429.7 1.8 fusion.28
  431.6 1.8 fusion.29
  433.5 0.0 copy-start
  433.5 1.9 select_subtract_fusion
  435.3 2.1 convolution_divide_fusion
  437.4 0.0 copy-done
  437.4 1.4 convolution_multiply_fusion.3
  (4 shorter events, 0.1 us)
Async XLA Ops:
  6.5 79.7 %all-gather.4.cloned.1.call-start = ((), (), s32[]{:S(2)}) async-start(), calls=%async_computation.1 | async-start | bytes 2228224 | tf_op jit(solution)/shard_map/all_gather | solution.py:47
  7.3 151.1 %reduce-scatter.2.cloned.1.call-start = ((), (), s32[]{:S(2)}) async-start(), calls=%async_computation.2 | async-start | bytes 4456448 | tf_op jit(solution)/shard_map/reduce_scatter | solution.py:51
  102.3 317.4 %all-reduce.2.cloned.1.call-start = ((), (), s32[]{:S(2)}) async-start(), calls=%async_computation.3 | async-start | bytes 2097152 | tf_op jit(solution)/shard_map/psum | solution.py:57
  419.8 6.2 %copy-start.1 = (f32[512,512]{1,0:T(8,128)S(1)}, f32[512,512]{1,0:T(8,128)}, u32[]{:S(2)}) copy-start(f32[512,512]{1,0:T(8,128)} %all-reduce.2.cloned.1.call-done) | copy-start | bytes 3145732
  433.5 3.9 copy-start
Sparse Core Ops, SparseCore 0:
  9.8 52.9 all-gather.3
  102.5 55.8 reduce-scatter.1
  163.8 255.8 all-reduce.1
where the time goes:
time: 446 us; the launch traced here: 445 us
  waiting for transfers between devices  315 us (71%)
  blocking collectives  78.8 us (18%)
  matrix products  35.2 us (8%)
  between operations  14 us (3%)
    psum x1, waiting for transfers between devices, per_device(): lax.psum(jnp.dot(own_rows.T, own_rows, precision=highest), ('row', 'col'))  258 us
    reduce_scatter x1, waiting for transfers between devices, per_device(): lax.psum_scatter(jnp.dot(kernel_block, stripe_rows, preferred_element_typ...  55.8 us
    all_gather x1, blocking collectives, per_device(): lax.all_gather(amplitude, 'col', axis=0, tiled=True)  25 us
    all_gather x1, blocking collectives, per_device(): lax.all_gather(points, 'col', axis=1, tiled=True)  18.8 us
    all_gather x1, blocking collectives, per_device(): lax.all_gather(points, 'row', axis=1, tiled=True)  17.7 us
    all_gather x1, blocking collectives, per_device(): lax.all_gather(amplitude, 'row', axis=0, tiled=True)  17.2 us
    dot_general x1, matrix products, per_device(): jnp.dot(kernel_block, stripe_rows, preferred_element_type=jnp.float32)  16.1 us
  transfers between devices with their start and end apart: 3, of which 2 were waited for; matrix products, arithmetic and copies ran while one was open for 0% of the time, Pallas kernels for 0%

commit v1 on v0

v1 whole, which is shorter than its diff:
```python
import math

import jax
import jax.numpy as jnp
from jax import lax
from jax.experimental import pallas as pl
from jax.experimental.pallas import tpu as pltpu
from jax.sharding import PartitionSpec as P

NS_ITERS = 3
CORRELATION = 4.0

MESH = pl.DeviceIdType.MESH
NX, NY, NZ, NCORE = 4, 4, 8, 2
PTS = 128
RANK = 512
WIDTH = 256
PARTS = RANK // WIDTH
ROWS = NZ * PTS
COLS = NX * NY * NCORE * PTS
FEATS = 48
OFFSETS = (4, 3, -3, 2, -2, 1, -1, 0)
SLOT = {off: i for i, off in enumerate(OFFSETS)}
UP = ((4, 0), (3, 1), (3, 0), (2, 1), (2, 0), (1, 1), (1, 0))
DOWN = ((4, 1), (-3, 0), (-3, 1), (-2, 0), (-2, 1), (-1, 0), (-1, 1))
BLOCKS = (
    ((0, 0), (0, 1), (0, 2), (0, 3), (1, 1)),
    ((1, 2), (1, 3), (2, 2), (2, 3), (3, 3)),
)
PLANE = tuple((dy, dx) for dy in range(NY) for dx in range(NX) if (dy, dx) != (0, 0))


def three_parts(v):
    high = v.astype(jnp.bfloat16).astype(jnp.float32)
    rest = v - high
    mid = rest.astype(jnp.bfloat16).astype(jnp.float32)
    low = (rest - mid).astype(jnp.bfloat16).astype(jnp.float32)
    return high, mid, low


def kernel(
    points,
    amplitude,
    sketch,
    out,
    row_pack,
    col_pack,
    row_packs,
    col_packs,
    row_feats,
    row_level,
    col_feats,
    col_level,
    tile,
    stripe,
    partial,
    up_in,
    down_in,
    basis,
    gram_part,
    plane_in,
    plane_sum,
    line_in,
    line_sum,
    gram_half,
    gram,
    square,
    polynomial,
    pack_sems,
    stripe_sems,
    ring_sems,
    basis_sems,
    gram_sems,
):
    row = lax.axis_index("row")
    col = lax.axis_index("col")
    y, x = lax.div(row, NX), lax.rem(row, NX)
    z, core = lax.div(col, NCORE), lax.rem(col, NCORE)

    def device(dy=0, dx=0, dz=0, dcore=0):
        return (
            lax.rem(y + dy + NY, NY) * NX + lax.rem(x + dx + NX, NX),
            lax.rem(z + dz + NZ, NZ) * NCORE + lax.rem(core + dcore, NCORE),
        )

    def send(src, dst, sems, index, to):
        copy = pltpu.make_async_remote_copy(
            src_ref=src,
            dst_ref=dst,
            send_sem=sems.at[0, index],
            recv_sem=sems.at[1, index],
            device_id=to,
            device_id_type=MESH,
        )
        copy.start()
        started.append(copy)
        return copy

    started = []
    other = device(dcore=1)

    barrier = pltpu.get_barrier_semaphore()
    for dy, dx in PLANE:
        pl.semaphore_signal(barrier, inc=1, device_id=device(dy=dy, dx=dx), device_id_type=MESH)
    for dz in range(1, NZ):
        pl.semaphore_signal(barrier, inc=1, device_id=device(dz=dz), device_id_type=MESH)
    pl.semaphore_signal(barrier, inc=1, device_id=other, device_id_type=MESH)

    weight = 0.5 / math.sqrt(ROWS * NX * NY * NCORE)
    per_unit = 1.0 / (CORRELATION * math.log(2.0))
    amp = amplitude[...]
    level = jnp.log(amp) * (1.0 / math.log(2.0)) + 0.5 * math.log2(weight)
    ux = (points[0:1, :] - 0.5) * per_unit
    uy = (points[1:2, :] - 0.5) * per_unit
    uz = (points[2:3, :] - 4.0) * per_unit
    norm = ux * ux + uy * uy + uz * uz
    row_pack[...] = jnp.zeros_like(row_pack)
    col_pack[...] = jnp.zeros_like(col_pack)
    for i, v in enumerate((ux, uy, uz)):
        row_pack[i : i + 1, :] = v
        col_pack[i : i + 1, :] = -2.0 * v
    row_pack[3:4, :] = norm
    row_pack[4:5, :] = jnp.ones_like(norm)
    row_pack[5:6, :] = level
    col_pack[3:4, :] = jnp.ones_like(norm)
    col_pack[4:5, :] = norm
    col_pack[6:7, :] = level
    row_packs[SLOT[0]] = row_pack[...]
    col_packs[0, 0, 0] = col_pack[...]
    for t in range(4):
        stripe[t, 0, 0, 0] = sketch[:, t * 128 : (t + 1) * 128]

    pl.semaphore_wait(barrier, len(PLANE) + NZ)

    line_packs = []
    for dz in range(1, NZ):
        at = SLOT[-dz if dz <= 3 else 8 - dz]
        line_packs.append(
            send(row_pack, row_packs.at[at], pack_sems, at, device(dz=dz))
        )
    plane_packs = []
    for dy, dx in PLANE:
        at = (-dy % NY, -dx % NX)
        plane_packs.append(
            send(
                col_pack,
                col_packs.at[0, at[0], at[1]],
                pack_sems,
                8 + at[0] * NX + at[1],
                device(dy=dy, dx=dx),
            )
        )
    first = {}
    for t in range(4):
        first[t] = []
        for d in range(1, 4):
            if t % 2 == 0:
                dst, to = stripe.at[t, 0, 0, -d % NX], device(dx=d)
            else:
                dst, to = stripe.at[t, 0, -d % NY, 0], device(dy=d)
            src = sketch.at[:, t * 128 : (t + 1) * 128]
            first[t].append(send(src, dst, stripe_sems, t * 8 + d, to))
    for copy in plane_packs:
        copy.wait_recv()
    pack_share = send(col_packs.at[0], col_packs.at[1], pack_sems, 8, other)
    second = {}
    for t in range(4):
        for copy in first[t]:
            copy.wait_recv()
        second[t] = []
        for d in range(1, 4):
            if t % 2 == 0:
                src, dst, to = stripe.at[t, 0, 0], stripe.at[t, 0, -d % NY], device(dy=d)
            else:
                src, dst, to = (
                    stripe.at[t, 0, :, 0],
                    stripe.at[t, 0, :, -d % NX],
                    device(dx=d),
                )
            second[t].append(send(src, dst, stripe_sems, t * 8 + 3 + d, to))
    for copy in line_packs:
        copy.wait_recv()

    def row_side(i, carry):
        pack = row_packs[i]
        high, mid, low = three_parts(pack)
        feats = jnp.concatenate([high, high, mid, high, low, mid], axis=0)
        feats = jnp.concatenate([feats, jnp.zeros((128 - FEATS, PTS), jnp.float32)], axis=0)
        at = pl.multiple_of(i * PTS, PTS)
        row_feats[pl.ds(at, PTS), :] = feats.T.astype(jnp.bfloat16)
        row_level[pl.ds(at, PTS), :] = jnp.broadcast_to(pack[5:6, :], (PTS, PTS)).T
        return carry

    lax.fori_loop(0, NZ, row_side, 0)
    pack_share.wait_recv()
    for k in range(NCORE):
        for dy in range(NY):
            for dx in range(NX):
                pack = col_packs[k, dy, dx]
                high, mid, low = three_parts(pack)
                feats = jnp.concatenate([high, mid, high, low, high, mid], axis=0)
                at = ((k * NY + dy) * NX + dx) * PTS
                col_feats[0:FEATS, at : at + PTS] = feats.astype(jnp.bfloat16)
                col_level[0:1, at : at + PTS] = pack[6:7, :]
    col_feats[FEATS:, :] = jnp.zeros((128 - FEATS, COLS), jnp.bfloat16)

    def kernel_rows(start, stop):
        def body(i, carry):
            at = pl.multiple_of(i * 512, 512)
            feats = col_feats[:, pl.ds(at, 512)]
            level = col_level[0:1, pl.ds(at, 512)]
            for m in range(start, stop, PTS):
                distance = jnp.dot(
                    row_feats[m : m + PTS, :], feats, preferred_element_type=jnp.float32
                )
                distance = jnp.maximum(distance, 1e-30)
                root = distance * lax.rsqrt(distance)
                levels = jnp.concatenate([row_level[m : m + PTS, :]] * 4, axis=1) + level
                tile[m : m + PTS, pl.ds(at, 512)] = jnp.exp2(levels - root).astype(jnp.bfloat16)
            return carry

        lax.fori_loop(0, COLS // 512, body, 0)

    kernel_rows(0, 3 * PTS)
    kernel_rows(3 * PTS, ROWS)
    own = slice(SLOT[0] * PTS, SLOT[0] * PTS + PTS)
    on_diagonal = lax.broadcasted_iota(jnp.int32, (PTS, PTS), 0) == lax.broadcasted_iota(
        jnp.int32, (PTS, PTS), 1
    )
    diagonal = weight * amp * amp + 1.0
    tile[own, 0:PTS] = jnp.where(
        on_diagonal, jnp.broadcast_to(diagonal, (PTS, PTS)), tile[own, 0:PTS].astype(jnp.float32)
    ).astype(jnp.bfloat16)

    up, down = {}, {}

    def share(h):
        copies = []
        for t in (2 * h, 2 * h + 1):
            for copy in second[t]:
                copy.wait_recv()
            copies.append(send(stripe.at[t, 0], stripe.at[t, 1], stripe_sems, t * 8, other))
        return copies

    def product(h, start, stop):
        right = jnp.concatenate(
            [stripe[2 * h].reshape(COLS, 128), stripe[2 * h + 1].reshape(COLS, 128)], axis=1
        )
        value = jnp.dot(
            tile[start * PTS : stop * PTS, :], right, preferred_element_type=jnp.float32
        )
        partial[h, start:stop] = value.reshape(stop - start, PTS, WIDTH)

    def half_of(h, off, half):
        return partial.at[h, SLOT[off], half * 64 : half * 64 + 64]

    def pass_on(h, i):
        for sends, plan, arrived, dz, base in (
            (up, UP, up_in, 1, 0),
            (down, DOWN, down_in, -1, 7),
        ):
            off, half = plan[i]
            mine = half_of(h, off, half)
            if i >= 2:
                sends[h, i - 2].wait_recv()
                mine[...] += arrived[h, i - 2]
            sends[h, i] = send(mine, arrived.at[h, i], ring_sems, h * 14 + base + i, device(dz=dz))

    def begin(h):
        for copy in share(h):
            copy.wait_recv()
        product(h, 0, 3)
        pass_on(h, 0)
        pass_on(h, 1)
        product(h, 3, 8)

    basis_copies = []

    def finish(h):
        for i, (a, b) in ((5, (1, 0)), (6, (0, 1))):
            up[h, i].wait_recv()
            half_of(h, 0, a)[...] += up_in[h, i]
            down[h, i].wait_recv()
            half_of(h, 0, b)[...] += down_in[h, i]
        where = slice(h * WIDTH, (h + 1) * WIDTH)
        basis[0, :, where] = partial[h, SLOT[0]]
        basis_copies.append(
            send(basis.at[0, :, where], basis.at[1, :, where], basis_sems, h, other)
        )

    begin(0)
    pass_on(0, 2)
    pass_on(0, 3)
    begin(1)
    pass_on(0, 4)
    pass_on(0, 5)
    pass_on(1, 2)
    pass_on(1, 3)
    pass_on(0, 6)
    pass_on(1, 4)
    pass_on(1, 5)
    finish(0)
    pass_on(1, 6)
    finish(1)
    for copy in basis_copies:
        copy.wait_recv()

    def columns(i):
        at = pl.multiple_of(i * 128, 128)
        return jnp.concatenate([basis[0, :, pl.ds(at, 128)], basis[1, :, pl.ds(at, 128)]], axis=0)

    for b, ((i0, j0), (i1, j1)) in enumerate(zip(*BLOCKS)):
        gram_part[:, b * 128 : (b + 1) * 128] = lax.dot_general(
            columns(i0 + core * (i1 - i0)),
            columns(j0 + core * (j1 - j0)),
            (((0,), (0,)), ((), ())),
            precision=lax.Precision.HIGH,
            preferred_element_type=jnp.float32,
        )

    def slice_at(r):
        return pl.ds(pl.multiple_of(r * 8, 8), 8)

    copies = []
    for dy, dx in PLANE:
        to = device(dy=dy, dx=dx)
        at = (-dy % NY) * NX + (-dx % NX)
        copies.append(
            send(gram_part.at[slice_at(to[0])], plane_in.at[at], gram_sems, at, to)
        )
    total = gram_part[slice_at(row), :]
    for i, copy in enumerate(copies):
        copy.wait_recv()
    for at in range(1, 16):
        total += plane_in[at]
    plane_sum[...] = total
    copies = []
    for dz in range(1, NZ):
        copies.append(
            send(plane_sum, line_in.at[NZ - dz], gram_sems, 16 + NZ - dz, device(dz=dz))
        )
    for copy in copies:
        copy.wait_recv()
    for at in range(1, NZ):
        total += line_in[at]
    line_sum[...] = total
    gram_half[core, slice_at(row), :] = total
    copies = []
    for dy, dx in PLANE:
        at = (-dy % NY) * NX + (-dx % NX)
        copies.append(
            send(
                line_sum,
                gram_half.at[core, slice_at(row)],
                gram_sems,
                24 + at,
                device(dy=dy, dx=dx),
            )
        )
    for copy in copies:
        copy.wait_recv()
    copy = send(gram_half.at[core], gram_half.at[core], gram_sems, 0, other)
    copy.wait_recv()

    norm_square = jnp.zeros((8, 128), jnp.float32)
    for k in range(NCORE):
        for b, (i, j) in enumerate(BLOCKS[k]):
            block = gram_half[k, :, b * 128 : (b + 1) * 128]
            gram[i * 128 : i * 128 + 128, j * 128 : j * 128 + 128] = block
            if i != j:
                gram[j * 128 : j * 128 + 128, i * 128 : i * 128 + 128] = block.T
            squares = jnp.sum((block * block).reshape(16, 8, 128), axis=0)
            norm_square += squares if i == j else 2.0 * squares
    scale = jnp.sqrt(jnp.sum(jnp.sum(norm_square, axis=0, keepdims=True), axis=1, keepdims=True))

    def dot(a, b):
        return jnp.dot(
            a, b, precision=lax.Precision.HIGH, preferred_element_type=jnp.float32
        )

    gram[...] = gram[...] * (1.0 / scale)
    square[...] = dot(gram[...], gram[...])
    inner = 0.0625 * square[...] - 0.5625 * gram[...]
    unit = (
        lax.broadcasted_iota(jnp.int32, (RANK, RANK), 0)
        == lax.broadcasted_iota(jnp.int32, (RANK, RANK), 1)
    ).astype(jnp.float32)
    polynomial[...] = (
        dot(square[...], inner + 1.6875 * unit) - 2.4375 * gram[...] + 2.25 * unit
    )
    start = dot(basis[0], polynomial[...])
    step = dot(start, gram[...])
    step = dot(step, polynomial[...])
    step = dot(step, polynomial[...])
    out[...] = (1.5 * start - 0.5 * step) * (math.sqrt(RANK) * lax.rsqrt(scale))

    for copy in started:
        copy.wait_send()


def per_device(points, amplitude, sketch):
    f32, bf16 = jnp.float32, jnp.bfloat16
    vmem = pl.BlockSpec(memory_space=pltpu.VMEM)
    return pl.pallas_call(
        kernel,
        out_shape=jax.ShapeDtypeStruct((PTS, RANK), f32),
        in_specs=[vmem] * 3,
        out_specs=vmem,
        scratch_shapes=[
            pltpu.VMEM((8, PTS), f32),
            pltpu.VMEM((8, PTS), f32),
            pltpu.VMEM((NZ, 8, PTS), f32),
            pltpu.VMEM((NCORE, NY, NX, 8, PTS), f32),
            pltpu.VMEM((ROWS, 128), bf16),
            pltpu.VMEM((ROWS, 128), f32),
            pltpu.VMEM((128, COLS), bf16),
            pltpu.VMEM((8, COLS), f32),
            pltpu.VMEM((ROWS, COLS), bf16),
            pltpu.VMEM((4, NCORE, NY, NX, PTS, 128), bf16),
            pltpu.VMEM((PARTS, NZ, PTS, WIDTH), f32),
            pltpu.VMEM((PARTS, 7, 64, WIDTH), f32),
            pltpu.VMEM((PARTS, 7, 64, WIDTH), f32),
            pltpu.VMEM((NCORE, PTS, RANK), f32),
            pltpu.VMEM((128, 640), f32),
            pltpu.VMEM((16, 8, 640), f32),
            pltpu.VMEM((8, 640), f32),
            pltpu.VMEM((NZ, 8, 640), f32),
            pltpu.VMEM((8, 640), f32),
            pltpu.VMEM((NCORE, 128, 640), f32),
            pltpu.VMEM((RANK, RANK), f32),
            pltpu.VMEM((RANK, RANK), f32),
            pltpu.VMEM((RANK, RANK), f32),
            pltpu.SemaphoreType.DMA((2, 24)),
            pltpu.SemaphoreType.DMA((2, 32)),
            pltpu.SemaphoreType.DMA((2, 14 * PARTS)),
            pltpu.SemaphoreType.DMA((2, PARTS)),
            pltpu.SemaphoreType.DMA((2, 40)),
        ],
        compiler_params=pltpu.CompilerParams(
            collective_id=0, has_side_effects=True, vmem_limit_bytes=56 << 20
        ),
        cost_estimate=pl.CostEstimate(
            flops=7_000_000_000, bytes_accessed=1 << 20, transcendentals=8 << 20
        ),
        name="kl_modes",
    )(points, amplitude.reshape(1, -1), sketch)


def solution(mesh):
    in_specs = (P(None, ("row", "col")), P(("row", "col")), P(("row", "col"), None))
    out_specs = P(("row", "col"), None)
    return jax.shard_map(
        per_device, mesh=mesh, in_specs=in_specs, out_specs=out_specs, check_vma=False
    )
```

time: 446 us -> 88.5 us (0.20)
  waiting for transfers between devices: 315 us -> 0 us
  Pallas kernels: 0 us -> 86.7 us
  blocking collectives: 78.8 us -> 0 us
  matrix products: 35.2 us -> 0 us
  between operations: 14 us -> 0.01 us
    psum x1 -> x0, waiting for transfers between devices: 258 us -> none  [per_device(): lax.psum(jnp.dot(own_rows.T, own_rows, precision=highest), ('row', 'col'))]
    pallas_call x0 -> x1, Pallas kernels: none -> 86.7 us  [per_device(): pl.pallas_call(kernel, out_shape=jax.ShapeDtypeStruct((PTS, RANK), f32),...]
    all_gather x4 -> x0, blocking collectives: 78.8 us -> none  [the longest x1 25 us: per_device(): lax.all_gather(amplitude, 'col', axis=0, tiled=True)]
    reduce_scatter x1 -> x0, waiting for transfers between devices: 55.8 us -> none  [per_device(): lax.psum_scatter(jnp.dot(kernel_block, stripe_rows, preferred_element_typ...]
    dot_general x11 -> x0, matrix products: 35.2 us -> none  [the longest x1 16.1 us: per_device(): jnp.dot(kernel_block, stripe_rows, preferred_element_type=jnp.float32)]
  transfers between devices with their start and end apart: 3 -> 0, of which waited for: 2 -> 0; matrix products, arithmetic and copies ran while one was open for 0% -> 0% of each run, Pallas kernels for 0% -> 0%
where the time goes in v1:
time: 88.5 us; the launch traced here: 88.4 us
  Pallas kernels  86.7 us (98%)
  local copies, waits for them, and re-layouts  1.67 us (2%)
    pallas_call x1, Pallas kernels, per_device(): pl.pallas_call(kernel, out_shape=jax.ShapeDtypeStruct((PTS, RANK), f32),...  86.7 us

profile of v1, /device:TPU:1, one launch (start us, length us, event | category | flops | bytes accessed | tf_op | source)
XLA Modules:
  0.0 88.4 jit_solution(7268673622057148800)
XLA Ops:
  0.0 86.7 %kl_modes.1 = f32[128,512]{1,0:T(8,128)} custom-call(f32[3,128]{1,0:T(4,128)} %points.1, f32[1,128]{1,0:T(1,128)} %bitcast.1, bf16[128,512]{1,0:T(8,128)(2,1)} %sketch.1), custom_call_target="tpu_custom_call" | custom-call | flops 7000000000 | bytes 1048576 | tf_op jit(solution)/shard_map/kl_modes/pallas_call | solution.py:404
  86.7 1.7 %copy.5 = f32[128,512]{1,0:T(8,128)} copy(f32[128,512]{1,0:T(8,128)} %kl_modes.1) | data formatting | bytes 524288

commit v2 on v1

v2 whole, which is shorter than its diff:
```python
import math

import jax
import jax.numpy as jnp
from jax import lax
from jax.experimental import pallas as pl
from jax.experimental.pallas import tpu as pltpu
from jax.sharding import PartitionSpec as P

NS_ITERS = 3
CORRELATION = 4.0

MESH = pl.DeviceIdType.MESH
NX, NY, NZ, NCORE = 4, 4, 8, 2
PTS = 128
RANK = 512
WIDTH = 128
PARTS = RANK // WIDTH
HALF = PTS // 2
ROWS = NZ * PTS
COLS = NX * NY * NCORE * PTS
FEATS = 48
OFFSETS = (4, 3, -3, 2, -2, 1, -1, 0)
SLOT = {off: i for i, off in enumerate(OFFSETS)}
UP = ((4, 0), (3, 1), (3, 0), (2, 1), (2, 0), (1, 1), (1, 0))
DOWN = ((4, 1), (-3, 0), (-3, 1), (-2, 0), (-2, 1), (-1, 0), (-1, 1))
BLOCKS = (
    ((0, 0), (0, 1), (1, 1), (0, 3), (1, 3)),
    ((0, 2), (1, 2), (2, 2), (2, 3), (3, 3)),
)
GROUPS = ((0, 3), (3, 5))
ORDER = (
    ("share", 0), ("kernel", 0, 1), ("kernel", 1, 3), ("share", 1), ("first", 0), ("second", 0),
    ("kernel", 3, 5), ("share", 2), ("first", 1), ("second", 1), ("pass", 0, 2), ("share", 3),
    ("first", 2), ("second", 2), ("third", 0), ("pass", 0, 3), ("first", 3), ("pass", 1, 2),
    ("second", 3), ("third", 1), ("pass", 0, 4), ("pass", 1, 3), ("third", 2), ("pass", 2, 2),
    ("pass", 2, 3), ("third", 3), ("kernel", 5, 7), ("pass", 1, 4), ("pass", 3, 2), ("kernel", 7, 8),
    ("pass", 3, 3), ("fourth", 0), ("pass", 0, 5), ("pass", 0, 6), ("last", 0), ("pass", 2, 4),
    ("fourth", 1), ("pass", 1, 5), ("last", 1), ("fourth", 2), ("pass", 1, 6), ("pass", 2, 5),
    ("pass", 3, 4), ("last", 2), ("fourth", 3), ("pass", 3, 5), ("last", 3), ("finish", 0),
    ("pass", 2, 6), ("finish", 1), ("pass", 3, 6), ("finish", 2),
)
PLANE = tuple((dy, dx) for dy in range(NY) for dx in range(NX) if (dy, dx) != (0, 0))


def three_parts(v):
    high = v.astype(jnp.bfloat16).astype(jnp.float32)
    rest = v - high
    mid = rest.astype(jnp.bfloat16).astype(jnp.float32)
    low = (rest - mid).astype(jnp.bfloat16).astype(jnp.float32)
    return high, mid, low


def kernel(
    points,
    amplitude,
    sketch,
    out,
    row_pack,
    col_pack,
    row_packs,
    col_packs,
    row_feats,
    row_level,
    col_feats,
    col_level,
    tile,
    stripe,
    partial,
    up_in,
    down_in,
    basis,
    gram_part,
    plane_in,
    plane_sum,
    line_in,
    line_sum,
    gram_half,
    gram,
    square,
    polynomial,
    pack_sems,
    stripe_sems,
    ring_sems,
    basis_sems,
    gram_sems,
    ready,
):
    row = lax.axis_index("row")
    col = lax.axis_index("col")
    y, x = lax.div(row, NX), lax.rem(row, NX)
    z, core = lax.div(col, NCORE), lax.rem(col, NCORE)

    def device(dy=0, dx=0, dz=0, dcore=0):
        return (
            lax.rem(y + dy + NY, NY) * NX + lax.rem(x + dx + NX, NX),
            lax.rem(z + dz + NZ, NZ) * NCORE + lax.rem(core + dcore + NCORE, NCORE),
        )

    def send(src, dst, sems, index, to):
        copy = pltpu.make_async_remote_copy(
            src_ref=src,
            dst_ref=dst,
            send_sem=sems.at[0, index],
            recv_sem=sems.at[1, index],
            device_id=to,
            device_id_type=MESH,
        )
        copy.start()
        started.append(copy)
        return copy

    started = []
    other = device(dcore=1)

    barrier = pltpu.get_barrier_semaphore()

    def report(to_core, **where):
        pl.semaphore_signal(
            barrier, inc=1, device_id=device(dcore=to_core - core, **where), device_id_type=MESH
        )

    for d in range(1, 4):
        report(0, dx=d)
        report(0, dy=d)
    pl.semaphore_signal(barrier, inc=1, device_id=other, device_id_type=MESH)
    for dz in range(1, NZ):
        report(1, dz=dz)

    weight = 0.5 / math.sqrt(ROWS * NX * NY * NCORE)
    per_unit = 1.0 / (CORRELATION * math.log(2.0))
    amp = amplitude[...]
    level = jnp.log(amp) * (1.0 / math.log(2.0)) + 0.5 * math.log2(weight)
    ux = (points[0:1, :] - 0.5) * per_unit
    uy = (points[1:2, :] - 0.5) * per_unit
    uz = (points[2:3, :] - 4.0) * per_unit
    norm = ux * ux + uy * uy + uz * uz
    row_pack[...] = jnp.zeros_like(row_pack)
    col_pack[...] = jnp.zeros_like(col_pack)
    for i, v in enumerate((ux, uy, uz)):
        row_pack[i : i + 1, :] = v
        col_pack[i : i + 1, :] = -2.0 * v
    row_pack[3:4, :] = norm
    row_pack[4:5, :] = jnp.ones_like(norm)
    row_pack[5:6, :] = level
    col_pack[3:4, :] = jnp.ones_like(norm)
    col_pack[4:5, :] = norm
    col_pack[6:7, :] = level
    row_packs[SLOT[0]] = row_pack[...]
    col_packs[0, 0, 0] = col_pack[...]
    for t in range(4):
        stripe[t, 0, 0, 0] = sketch[:, t * 128 : (t + 1) * 128]

    @pl.when(core == 0)
    def _():
        pl.semaphore_wait(barrier, 13)
        pl.semaphore_signal(ready, inc=1, device_id=other, device_id_type=MESH)

    @pl.when(core == 1)
    def _():
        pl.semaphore_wait(ready, 1)

    near, far = slice(0, HALF), slice(HALF, PTS)

    def first_stage(t):
        copies = []
        where = slice(t * WIDTH, (t + 1) * WIDTH)
        for d in range(1, 4):
            copies.append(
                send(
                    sketch.at[near, where],
                    stripe.at[t, 0, 0, -d % NX, near],
                    stripe_sems,
                    t * 16 + d,
                    device(dx=d),
                )
            )
            copies.append(
                send(
                    sketch.at[far, where],
                    stripe.at[t, 0, -d % NY, 0, far],
                    stripe_sems,
                    t * 16 + 3 + d,
                    device(dy=d),
                )
            )
        return copies

    def second_stage(t):
        for copy in first[t]:
            copy.wait_recv()
        copies = []
        for d in range(1, 4):
            copies.append(
                send(
                    stripe.at[t, 0, 0, :, near],
                    stripe.at[t, 0, -d % NY, :, near],
                    stripe_sems,
                    t * 16 + 6 + d,
                    device(dy=d),
                )
            )
            copies.append(
                send(
                    stripe.at[t, 0, :, 0, far],
                    stripe.at[t, 0, :, -d % NX, far],
                    stripe_sems,
                    t * 16 + 9 + d,
                    device(dx=d),
                )
            )
        return copies

    packs_x = [
        send(col_pack, col_packs.at[0, 0, -d % NX], pack_sems, 8 + d, device(dx=d))
        for d in range(1, 4)
    ]
    first = {t: first_stage(t) for t in range(PARTS)}

    @pl.when(core == 1)
    def _():
        pl.semaphore_wait(barrier, 15)
        pl.semaphore_signal(ready, inc=1, device_id=other, device_id_type=MESH)

    @pl.when(core == 0)
    def _():
        pl.semaphore_wait(ready, 1)

    line_packs = []
    for dz in range(1, NZ):
        at = SLOT[-dz if dz <= 3 else 8 - dz]
        line_packs.append(send(row_pack, row_packs.at[at], pack_sems, at, device(dz=dz)))
    for copy in packs_x:
        copy.wait_recv()
    packs_y = [
        send(col_packs.at[0, 0], col_packs.at[0, -d % NY], pack_sems, 11 + d, device(dy=d))
        for d in range(1, 4)
    ]
    second = {t: second_stage(t) for t in range(PARTS)}
    for copy in packs_y:
        copy.wait_recv()
    pack_share = send(col_packs.at[0], col_packs.at[1], pack_sems, 8, other)

    def row_side(i, carry):
        pack = row_packs[i]
        high, mid, low = three_parts(pack)
        feats = jnp.concatenate([high, high, mid, high, low, mid], axis=0)
        feats = jnp.concatenate([feats, jnp.zeros((128 - FEATS, PTS), jnp.float32)], axis=0)
        at = pl.multiple_of(i * PTS, PTS)
        row_feats[pl.ds(at, PTS), :] = feats.T.astype(jnp.bfloat16)
        row_level[pl.ds(at, PTS), :] = jnp.broadcast_to(pack[5:6, :], (PTS, PTS)).T
        return carry

    def column_side(k):
        for dy in range(NY):
            for dx in range(NX):
                pack = col_packs[k, dy, dx]
                high, mid, low = three_parts(pack)
                feats = jnp.concatenate([high, mid, high, low, high, mid], axis=0)
                at = ((k * NY + dy) * NX + dx) * PTS
                col_feats[0:FEATS, at : at + PTS] = feats.astype(jnp.bfloat16)
                col_level[0:1, at : at + PTS] = pack[6:7, :]

    col_feats[FEATS:, :] = jnp.zeros((128 - FEATS, COLS), jnp.bfloat16)
    column_side(0)
    pack_share.wait_recv()
    column_side(1)
    for copy in line_packs:
        copy.wait_recv()
    lax.fori_loop(0, NZ, row_side, 0)

    def kernel_rows(start, stop):
        def body(i, carry):
            at = pl.multiple_of(i * 512, 512)
            feats = col_feats[:, pl.ds(at, 512)]
            level = col_level[0:1, pl.ds(at, 512)]
            for m in range(start, stop, PTS):
                distance = jnp.dot(
                    row_feats[m : m + PTS, :], feats, preferred_element_type=jnp.float32
                )
                distance = jnp.maximum(distance, 1e-30)
                root = distance * lax.rsqrt(distance)
                levels = jnp.concatenate([row_level[m : m + PTS, :]] * 4, axis=1) + level
                tile[m : m + PTS, pl.ds(at, 512)] = jnp.exp2(levels - root).astype(jnp.bfloat16)
            return carry

        lax.fori_loop(0, COLS // 512, body, 0)

    def place_diagonal():
        own = slice(SLOT[0] * PTS, SLOT[0] * PTS + PTS)
        on_diagonal = lax.broadcasted_iota(jnp.int32, (PTS, PTS), 0) == lax.broadcasted_iota(
            jnp.int32, (PTS, PTS), 1
        )
        diagonal = jnp.broadcast_to(weight * amp * amp + 1.0, (PTS, PTS))
        tile[own, 0:PTS] = jnp.where(
            on_diagonal, diagonal, tile[own, 0:PTS].astype(jnp.float32)
        ).astype(jnp.bfloat16)

    up, down, shares = {}, {}, {}

    def share(c):
        for copy in second[c]:
            copy.wait_recv()
        shares[c] = send(stripe.at[c, 0], stripe.at[c, 1], stripe_sems, c * 16, other)

    def block_product(c, start, stop):
        partial[c, start:stop] = jnp.dot(
            tile[start * PTS : stop * PTS, :],
            stripe[c].reshape(COLS, WIDTH),
            preferred_element_type=jnp.float32,
        ).reshape(stop - start, PTS, WIDTH)

    def half_of(c, off, half):
        return partial.at[c, SLOT[off], half * HALF : (half + 1) * HALF]

    def pass_on(c, *steps):
        for i in steps:
            for sends, plan, arrived, dz, base in (
                (up, UP, up_in, 1, 0),
                (down, DOWN, down_in, -1, 7),
            ):
                off, half = plan[i]
                mine = half_of(c, off, half)
                if i >= 2:
                    sends[c, i - 2].wait_recv()
                    mine[...] += arrived[c, i - 2]
                sends[c, i] = send(
                    mine, arrived.at[c, i], ring_sems, c * 14 + base + i, device(dz=dz)
                )

    def first_product(c):
        shares[c].wait_recv()
        block_product(c, 0, 1)
        pass_on(c, 0)

    def second_product(c):
        block_product(c, 1, 3)
        pass_on(c, 1)

    def kernel_blocks(start, stop):
        kernel_rows(start * PTS, stop * PTS)
        if stop == NZ:
            place_diagonal()

    basis_copies = []

    def finish(c):
        for i, (a, b) in ((5, (1, 0)), (6, (0, 1))):
            up[c, i].wait_recv()
            half_of(c, 0, a)[...] += up_in[c, i]
            down[c, i].wait_recv()
            half_of(c, 0, b)[...] += down_in[c, i]
        where = slice(c * WIDTH, (c + 1) * WIDTH)
        basis[0, :, where] = partial[c, SLOT[0]]
        basis_copies.append(
            send(basis.at[0, :, where], basis.at[1, :, where], basis_sems, c, other)
        )

    def columns(i):
        at = pl.multiple_of(i * 128, 128)
        return jnp.concatenate([basis[0, :, pl.ds(at, 128)], basis[1, :, pl.ds(at, 128)]], axis=0)

    def slice_at(r):
        return pl.ds(pl.multiple_of(r * 8, 8), 8)

    def lanes(g):
        return slice(GROUPS[g][0] * 128, GROUPS[g][1] * 128)

    def chip_blocks(g):
        for b in range(*GROUPS[g]):
            (i0, j0), (i1, j1) = BLOCKS[0][b], BLOCKS[1][b]
            gram_part[:, b * 128 : (b + 1) * 128] = lax.dot_general(
                columns(i0 + core * (i1 - i0)),
                columns(j0 + core * (j1 - j0)),
                (((0,), (0,)), ((), ())),
                precision=lax.Precision.HIGH,
                preferred_element_type=jnp.float32,
            )
        copies = []
        for dy, dx in PLANE:
            to = device(dy=dy, dx=dx)
            at = (-dy % NY) * NX + (-dx % NX)
            copies.append(
                send(
                    gram_part.at[slice_at(to[0]), lanes(g)],
                    plane_in.at[at, :, lanes(g)],
                    gram_sems,
                    g * 40 + at,
                    to,
                )
            )
        return copies

    def over_plane(g, copies):
        for copy in copies:
            copy.wait_recv()
        total = gram_part[slice_at(row), lanes(g)]
        for at in range(1, 16):
            total += plane_in[at, :, lanes(g)]
        plane_sum[:, lanes(g)] = total
        return [
            send(
                plane_sum.at[:, lanes(g)],
                line_in.at[NZ - dz, :, lanes(g)],
                gram_sems,
                g * 40 + 16 + NZ - dz,
                device(dz=dz),
            )
            for dz in range(1, NZ)
        ]

    def over_line(g, copies):
        for copy in copies:
            copy.wait_recv()
        total = plane_sum[:, lanes(g)]
        for at in range(1, NZ):
            total += line_in[at, :, lanes(g)]
        line_sum[:, lanes(g)] = total
        gram_half[core, slice_at(row), lanes(g)] = total
        return [
            send(
                line_sum.at[:, lanes(g)],
                gram_half.at[core, slice_at(row), lanes(g)],
                gram_sems,
                g * 40 + 24 + (-dy % NY) * NX + (-dx % NX),
                device(dy=dy, dx=dx),
            )
            for dy, dx in PLANE
        ]

    def to_other(g, copies):
        for copy in copies:
            copy.wait_recv()
        half = gram_half.at[core, :, lanes(g)]
        return send(half, half, gram_sems, g * 40, other)

    work = {
        "share": share,
        "kernel": kernel_blocks,
        "first": first_product,
        "second": second_product,
        "third": lambda c: block_product(c, 3, 5),
        "fourth": lambda c: block_product(c, 5, 7),
        "last": lambda c: block_product(c, 7, 8),
        "pass": pass_on,
        "finish": finish,
    }
    for name, *which in ORDER:
        work[name](*which)
    for copy in basis_copies:
        copy.wait_recv()
    early = chip_blocks(0)
    finish(3)
    basis_copies[3].wait_recv()
    late = chip_blocks(1)
    early = over_plane(0, early)
    late = over_plane(1, late)
    early = over_line(0, early)
    late = over_line(1, late)
    early = to_other(0, early)
    late = to_other(1, late)
    early.wait_recv()
    late.wait_recv()

    norm_square = jnp.zeros((8, 128), jnp.float32)
    for k in range(NCORE):
        for b, (i, j) in enumerate(BLOCKS[k]):
            block = gram_half[k, :, b * 128 : (b + 1) * 128]
            gram[i * 128 : i * 128 + 128, j * 128 : j * 128 + 128] = block
            if i != j:
                gram[j * 128 : j * 128 + 128, i * 128 : i * 128 + 128] = block.T
            squares = jnp.sum((block * block).reshape(16, 8, 128), axis=0)
            norm_square += squares if i == j else 2.0 * squares
    scale = jnp.sqrt(jnp.sum(jnp.sum(norm_square, axis=0, keepdims=True), axis=1, keepdims=True))

    def dot(a, b):
        return jnp.dot(
            a, b, precision=lax.Precision.HIGH, preferred_element_type=jnp.float32
        )

    gram[...] = gram[...] * (1.0 / scale)
    square[...] = dot(gram[...], gram[...])
    inner = 0.0625 * square[...] - 0.5625 * gram[...]
    unit = (
        lax.broadcasted_iota(jnp.int32, (RANK, RANK), 0)
        == lax.broadcasted_iota(jnp.int32, (RANK, RANK), 1)
    ).astype(jnp.float32)
    polynomial[...] = (
        dot(square[...], inner + 1.6875 * unit) - 2.4375 * gram[...] + 2.25 * unit
    )
    start = dot(basis[0], polynomial[...])
    step = dot(start, gram[...])
    step = dot(step, polynomial[...])
    step = dot(step, polynomial[...])
    out[...] = (1.5 * start - 0.5 * step) * (math.sqrt(RANK) * lax.rsqrt(scale))

    for copy in started:
        copy.wait_send()


def per_device(points, amplitude, sketch):
    f32, bf16 = jnp.float32, jnp.bfloat16
    vmem = pl.BlockSpec(memory_space=pltpu.VMEM)
    return pl.pallas_call(
        kernel,
        out_shape=jax.ShapeDtypeStruct((PTS, RANK), f32),
        in_specs=[vmem] * 3,
        out_specs=vmem,
        scratch_shapes=[
            pltpu.VMEM((8, PTS), f32),
            pltpu.VMEM((8, PTS), f32),
            pltpu.VMEM((NZ, 8, PTS), f32),
            pltpu.VMEM((NCORE, NY, NX, 8, PTS), f32),
            pltpu.VMEM((ROWS, 128), bf16),
            pltpu.VMEM((ROWS, 128), f32),
            pltpu.VMEM((128, COLS), bf16),
            pltpu.VMEM((8, COLS), f32),
            pltpu.VMEM((ROWS, COLS), bf16),
            pltpu.VMEM((PARTS, NCORE, NY, NX, PTS, WIDTH), bf16),
            pltpu.VMEM((PARTS, NZ, PTS, WIDTH), f32),
            pltpu.VMEM((PARTS, 7, HALF, WIDTH), f32),
            pltpu.VMEM((PARTS, 7, HALF, WIDTH), f32),
            pltpu.VMEM((NCORE, PTS, RANK), f32),
            pltpu.VMEM((128, 640), f32),
            pltpu.VMEM((16, 8, 640), f32),
            pltpu.VMEM((8, 640), f32),
            pltpu.VMEM((NZ, 8, 640), f32),
            pltpu.VMEM((8, 640), f32),
            pltpu.VMEM((NCORE, 128, 640), f32),
            pltpu.VMEM((RANK, RANK), f32),
            pltpu.VMEM((RANK, RANK), f32),
            pltpu.VMEM((RANK, RANK), f32),
            pltpu.SemaphoreType.DMA((2, 24)),
            pltpu.SemaphoreType.DMA((2, 16 * PARTS)),
            pltpu.SemaphoreType.DMA((2, 14 * PARTS)),
            pltpu.SemaphoreType.DMA((2, PARTS)),
            pltpu.SemaphoreType.DMA((2, 80)),
            pltpu.SemaphoreType.REGULAR,
        ],
        compiler_params=pltpu.CompilerParams(
            collective_id=0, has_side_effects=True, vmem_limit_bytes=56 << 20
        ),
        cost_estimate=pl.CostEstimate(
            flops=7_000_000_000, bytes_accessed=1 << 20, transcendentals=8 << 20
        ),
        name="kl_modes",
    )(points, amplitude.reshape(1, -1), sketch)


def solution(mesh):
    in_specs = (P(None, ("row", "col")), P(("row", "col")), P(("row", "col"), None))
    out_specs = P(("row", "col"), None)
    return jax.shard_map(
        per_device, mesh=mesh, in_specs=in_specs, out_specs=out_specs, check_vma=False
    )
```

time: 88.5 us -> 81.6 us (0.922)
  Pallas kernels: 86.7 us -> 79.8 us
    pallas_call x1, Pallas kernels: 86.7 us -> 79.8 us  [per_device(): pl.pallas_call(kernel, out_shape=jax.ShapeDtypeStruct((PTS, RANK), f32),...]
where the time goes in v2:
time: 81.6 us; the launch traced here: 81.4 us
  Pallas kernels  79.8 us (98%)
  local copies, waits for them, and re-layouts  1.67 us (2%)
    pallas_call x1, Pallas kernels, per_device(): pl.pallas_call(kernel, out_shape=jax.ShapeDtypeStruct((PTS, RANK), f32),...  79.8 us
    unnamed x1, local copies, waits for them, and re-layouts  1.67 us

profile of v2, /device:TPU:1, one launch (start us, length us, event | category | flops | bytes accessed | tf_op | source)
XLA Modules:
  0.0 81.4 jit_solution(5538112844902021992)
XLA Ops:
  0.0 79.8 %kl_modes.1 = f32[128,512]{1,0:T(8,128)} custom-call(f32[3,128]{1,0:T(4,128)} %points.1, f32[1,128]{1,0:T(1,128)} %bitcast.1, bf16[128,512]{1,0:T(8,128)(2,1)} %sketch.1), custom_call_target="tpu_custom_call" | custom-call | flops 7000000000 | bytes 1048576 | tf_op jit(solution)/shard_map/kl_modes/pallas_call | solution.py:504
  79.8 1.7 %copy.5 = f32[128,512]{1,0:T(8,128)} copy(f32[128,512]{1,0:T(8,128)} %kl_modes.1) | data formatting | bytes 524288

commit v3 on v2

--- a/solution.py
+++ b/solution.py
@@ -17,6 +17,7 @@
 WIDTH = 128
 PARTS = RANK // WIDTH
 HALF = PTS // 2
+LANES = 1024
 ROWS = NZ * PTS
 COLS = NX * NY * NCORE * PTS
 FEATS = 48
@@ -30,17 +31,22 @@
 )
 GROUPS = ((0, 3), (3, 5))
 ORDER = (
-    ("share", 0), ("kernel", 0, 1), ("kernel", 1, 3), ("share", 1), ("first", 0), ("second", 0),
-    ("kernel", 3, 5), ("share", 2), ("first", 1), ("second", 1), ("pass", 0, 2), ("share", 3),
-    ("first", 2), ("second", 2), ("third", 0), ("pass", 0, 3), ("first", 3), ("pass", 1, 2),
-    ("second", 3), ("third", 1), ("pass", 0, 4), ("pass", 1, 3), ("third", 2), ("pass", 2, 2),
-    ("pass", 2, 3), ("third", 3), ("kernel", 5, 7), ("pass", 1, 4), ("pass", 3, 2), ("kernel", 7, 8),
-    ("pass", 3, 3), ("fourth", 0), ("pass", 0, 5), ("pass", 0, 6), ("last", 0), ("pass", 2, 4),
-    ("fourth", 1), ("pass", 1, 5), ("last", 1), ("fourth", 2), ("pass", 1, 6), ("pass", 2, 5),
-    ("pass", 3, 4), ("last", 2), ("fourth", 3), ("pass", 3, 5), ("last", 3), ("finish", 0),
-    ("pass", 2, 6), ("finish", 1), ("pass", 3, 6), ("finish", 2),
+    ("kernel", 0, 1), ("share", 0), ("share", 1), ("kernel", 1, 3), ("first", 0), ("first", 1),
+    ("share", 2), ("second", 0), ("second", 1), ("first", 2), ("second", 2), ("kernel", 3, 5),
+    ("pass", 1, 2), ("share", 3), ("pass", 0, 2), ("third", 0), ("pass", 0, 3), ("pass", 1, 3),
+    ("first", 3), ("pass", 2, 2), ("second", 3), ("kernel", 5, 7), ("pass", 0, 4), ("pass", 1, 4),
+    ("fourth", 0), ("pass", 1, 5), ("pass", 0, 5), ("pass", 3, 2), ("third", 1), ("pass", 2, 3),
+    ("pass", 2, 4), ("pass", 3, 3), ("fourth", 1), ("pass", 0, 6), ("last", 1), ("pass", 1, 6),
+    ("last", 0), ("pass", 3, 4), ("pass", 2, 5), ("pass", 2, 6), ("pass", 3, 5), ("finish", 0),
+    ("finish", 1), ("pass", 3, 6), ("finish", 2),
 )
-PLANE = tuple((dy, dx) for dy in range(NY) for dx in range(NX) if (dy, dx) != (0, 0))
+PLANE = tuple(
+    sorted(
+        ((dy, dx) for dy in range(NY) for dx in range(NX) if (dy, dx) != (0, 0)),
+        key=lambda p: -(min(p[0], NY - p[0]) + min(p[1], NX - p[1])),
+    )
+)
+LINE = tuple(sorted(range(1, NZ), key=lambda d: -min(d, NZ - d)))
 
 
 def three_parts(v):
@@ -120,12 +126,12 @@
             barrier, inc=1, device_id=device(dcore=to_core - core, **where), device_id_type=MESH
         )
 
+    for dz in LINE:
+        report(1, dz=dz)
     for d in range(1, 4):
         report(0, dx=d)
         report(0, dy=d)
     pl.semaphore_signal(barrier, inc=1, device_id=other, device_id_type=MESH)
-    for dz in range(1, NZ):
-        report(1, dz=dz)
 
     weight = 0.5 / math.sqrt(ROWS * NX * NY * NCORE)
     per_unit = 1.0 / (CORRELATION * math.log(2.0))
@@ -227,7 +233,7 @@
         pl.semaphore_wait(ready, 1)
 
     line_packs = []
-    for dz in range(1, NZ):
+    for dz in LINE:
         at = SLOT[-dz if dz <= 3 else 8 - dz]
         line_packs.append(send(row_pack, row_packs.at[at], pack_sems, at, device(dz=dz)))
     for copy in packs_x:
@@ -265,26 +271,26 @@
     column_side(0)
     pack_share.wait_recv()
     column_side(1)
-    for copy in line_packs:
-        copy.wait_recv()
-    lax.fori_loop(0, NZ, row_side, 0)
+    row_side(SLOT[0], 0)
 
     def kernel_rows(start, stop):
         def body(i, carry):
-            at = pl.multiple_of(i * 512, 512)
-            feats = col_feats[:, pl.ds(at, 512)]
-            level = col_level[0:1, pl.ds(at, 512)]
+            at = pl.multiple_of(i * LANES, LANES)
+            feats = col_feats[:, pl.ds(at, LANES)]
+            level = col_level[0:1, pl.ds(at, LANES)]
             for m in range(start, stop, PTS):
                 distance = jnp.dot(
                     row_feats[m : m + PTS, :], feats, preferred_element_type=jnp.float32
                 )
                 distance = jnp.maximum(distance, 1e-30)
                 root = distance * lax.rsqrt(distance)
-                levels = jnp.concatenate([row_level[m : m + PTS, :]] * 4, axis=1) + level
-                tile[m : m + PTS, pl.ds(at, 512)] = jnp.exp2(levels - root).astype(jnp.bfloat16)
+                levels = jnp.concatenate([row_level[m : m + PTS, :]] * (LANES // PTS), axis=1)
+                tile[m : m + PTS, pl.ds(at, LANES)] = jnp.exp2(levels + level - root).astype(
+                    jnp.bfloat16
+                )
             return carry
 
-        lax.fori_loop(0, COLS // 512, body, 0)
+        lax.fori_loop(0, COLS // LANES, body, 0)
 
     def place_diagonal():
         own = slice(SLOT[0] * PTS, SLOT[0] * PTS + PTS)
@@ -295,6 +301,12 @@
         tile[own, 0:PTS] = jnp.where(
             on_diagonal, diagonal, tile[own, 0:PTS].astype(jnp.float32)
         ).astype(jnp.bfloat16)
+
+    kernel_rows(SLOT[0] * PTS, NZ * PTS)
+    place_diagonal()
+    for copy in line_packs:
+        copy.wait_recv()
+    lax.fori_loop(0, SLOT[0], row_side, 0)
 
     up, down, shares = {}, {}, {}
 
@@ -309,6 +321,18 @@
             stripe[c].reshape(COLS, WIDTH),
             preferred_element_type=jnp.float32,
         ).reshape(stop - start, PTS, WIDTH)
+
+    def pair_product(p, start, stop):
+        chunks = (2 * p, 2 * p + 1)
+        value = jnp.dot(
+            tile[start * PTS : stop * PTS, :],
+            jnp.concatenate([stripe[c].reshape(COLS, WIDTH) for c in chunks], axis=1),
+            preferred_element_type=jnp.float32,
+        )
+        for i, c in enumerate(chunks):
+            partial[c, start:stop] = value[:, i * WIDTH : (i + 1) * WIDTH].reshape(
+                stop - start, PTS, WIDTH
+            )
 
     def half_of(c, off, half):
         return partial.at[c, SLOT[off], half * HALF : (half + 1) * HALF]
@@ -336,11 +360,6 @@
     def second_product(c):
         block_product(c, 1, 3)
         pass_on(c, 1)
-
-    def kernel_blocks(start, stop):
-        kernel_rows(start * PTS, stop * PTS)
-        if stop == NZ:
-            place_diagonal()
 
     basis_copies = []
 
@@ -406,7 +425,7 @@
                 g * 40 + 16 + NZ - dz,
                 device(dz=dz),
             )
-            for dz in range(1, NZ)
+            for dz in LINE
         ]
 
     def over_line(g, copies):
@@ -436,12 +455,12 @@
 
     work = {
         "share": share,
-        "kernel": kernel_blocks,
+        "kernel": lambda a, b: kernel_rows(a * PTS, b * PTS),
         "first": first_product,
         "second": second_product,
-        "third": lambda c: block_product(c, 3, 5),
-        "fourth": lambda c: block_product(c, 5, 7),
-        "last": lambda c: block_product(c, 7, 8),
+        "third": lambda p: pair_product(p, 3, 5),
+        "fourth": lambda p: pair_product(p, 5, 7),
+        "last": lambda p: pair_product(p, 7, 8),
         "pass": pass_on,
         "finish": finish,
     }
@@ -538,7 +557,7 @@
             pltpu.SemaphoreType.REGULAR,
         ],
         compiler_params=pltpu.CompilerParams(
-            collective_id=0, has_side_effects=True, vmem_limit_bytes=56 << 20
+            collective_id=0, has_side_effects=True, vmem_limit_bytes=28 << 20
         ),
         cost_estimate=pl.CostEstimate(
             flops=7_000_000_000, bytes_accessed=1 << 20, transcendentals=8 << 20

time: 81.6 us -> 77.5 us (0.950)
  Pallas kernels: 79.8 us -> 74.4 us
  local copies, waits for them, and re-layouts: 1.67 us -> 2.94 us
    pallas_call x1, Pallas kernels: 79.8 us -> 74.4 us  [per_device(): pl.pallas_call(kernel, out_shape=jax.ShapeDtypeStruct((PTS, RANK), f32),...]
    unnamed x1 -> x7, local copies, waits for them, and re-layouts: 1.67 us -> 2.94 us
where the time goes in v3:
time: 77.5 us; the launch traced here: 77.4 us
  Pallas kernels  74.4 us (96%)
  local copies, waits for them, and re-layouts  2.94 us (4%)
    pallas_call x1, Pallas kernels, per_device(): pl.pallas_call(kernel, out_shape=jax.ShapeDtypeStruct((PTS, RANK), f32),...  74.4 us
    unnamed x7, local copies, waits for them, and re-layouts  2.94 us

profile of v3, /device:TPU:1, one launch (start us, length us, event | category | flops | bytes accessed | tf_op | source)
XLA Modules:
  0.0 77.4 jit_solution(16116010523395422312)
XLA Ops:
  0.0 0.0 copy-start.2
  0.0 0.7 copy-done.2
  0.7 0.0 copy-start
  0.7 0.9 %copy-done = bf16[128,512]{1,0:T(8,128)(2,1)S(1)} copy-done((bf16[128,512]{1,0:T(8,128)(2,1)S(1)}, bf16[128,512]{1,0:T(8,128)(2,1)}, u32[]{:S(2)}) %copy-start) | copy-done | bytes 131096
  1.6 0.0 copy-start.1
  1.6 0.7 copy-done.1
  2.2 74.4 %kl_modes.1 = f32[128,512]{1,0:T(8,128)S(1)} custom-call(f32[3,128]{1,0:T(4,128)S(1)} %copy-done.1, f32[1,128]{1,0:T(1,128)S(1)} %bitcast.1, bf16[128,512]{1,0:T(8,128)(2,1)S(1)} %copy-done), custom_call_target="tpu_custom_call" | custom-call | flops 7000000000 | bytes 1048576 | tf_op jit(solution)/shard_map/kl_modes/pallas_call | solution.py:523
  76.6 0.7 copy.5
Async XLA Ops:
  0.0 0.7 copy-start.2
  0.7 0.9 %copy-start = (bf16[128,512]{1,0:T(8,128)(2,1)S(1)}, bf16[128,512]{1,0:T(8,128)(2,1)}, u32[]{:S(2)}) copy-start(bf16[128,512]{1,0:T(8,128)(2,1)} %sketch.1) | copy-start | bytes 393220
  1.6 0.7 copy-start.1

commit v4 on v3

--- a/solution.py
+++ b/solution.py
@@ -468,16 +468,29 @@
         work[name](*which)
     for copy in basis_copies:
         copy.wait_recv()
+    def drain(count):
+        for copy in started[:count]:
+            copy.wait_send()
+        del started[:count]
+
+    ring_sends = len(started)
     early = chip_blocks(0)
     finish(3)
     basis_copies[3].wait_recv()
     late = chip_blocks(1)
+    block_sends = len(started) - ring_sends
+    drain(ring_sends)
     early = over_plane(0, early)
     late = over_plane(1, late)
+    drain(block_sends)
+    line_sends = len(started)
     early = over_line(0, early)
     late = over_line(1, late)
+    drain(line_sends)
+    plane_sends = len(started)
     early = to_other(0, early)
     late = to_other(1, late)
+    drain(plane_sends)
     early.wait_recv()
     late.wait_recv()
 
@@ -513,8 +526,7 @@
     step = dot(step, polynomial[...])
     out[...] = (1.5 * start - 0.5 * step) * (math.sqrt(RANK) * lax.rsqrt(scale))
 
-    for copy in started:
-        copy.wait_send()
+    drain(len(started))
 
 
 def per_device(points, amplitude, sketch):

time: 77.5 us -> 77.2 us (level)
  no operation moved by 1% of the time
where the time goes in v4:
time: 77.2 us; the launch traced here: 77 us
  Pallas kernels  74.1 us (96%)
  local copies, waits for them, and re-layouts  2.94 us (4%)
    pallas_call x1, Pallas kernels, per_device(): pl.pallas_call(kernel, out_shape=jax.ShapeDtypeStruct((PTS, RANK), f32),...  74.1 us
    unnamed x7, local copies, waits for them, and re-layouts  2.94 us

profile of v4, /device:TPU:1, one launch (start us, length us, event | category | flops | bytes accessed | tf_op | source)
XLA Modules:
  0.0 77.0 jit_solution(8166213025996639614)
XLA Ops:
  0.0 0.0 copy-start.2
  0.0 0.7 copy-done.2
  0.7 0.0 copy-start
  0.7 0.9 %copy-done = bf16[128,512]{1,0:T(8,128)(2,1)S(1)} copy-done((bf16[128,512]{1,0:T(8,128)(2,1)S(1)}, bf16[128,512]{1,0:T(8,128)(2,1)}, u32[]{:S(2)}) %copy-start) | copy-done | bytes 131096
  1.6 0.0 copy-start.1
  1.6 0.7 copy-done.1
  2.2 74.1 %kl_modes.1 = f32[128,512]{1,0:T(8,128)S(1)} custom-call(f32[3,128]{1,0:T(4,128)S(1)} %copy-done.1, f32[1,128]{1,0:T(1,128)S(1)} %bitcast.1, bf16[128,512]{1,0:T(8,128)(2,1)S(1)} %copy-done), custom_call_target="tpu_custom_call" | custom-call | flops 7000000000 | bytes 1048576 | tf_op jit(solution)/shard_map/kl_modes/pallas_call | solution.py:535
  76.3 0.7 copy.5
Async XLA Ops:
  0.0 0.7 copy-start.2
  0.7 0.9 %copy-start = (bf16[128,512]{1,0:T(8,128)(2,1)S(1)}, bf16[128,512]{1,0:T(8,128)(2,1)}, u32[]{:S(2)}) copy-start(bf16[128,512]{1,0:T(8,128)(2,1)} %sketch.1) | copy-start | bytes 393220
  1.6 0.7 copy-start.1

commit v5 on v4

--- a/solution.py
+++ b/solution.py
@@ -62,6 +62,7 @@
     amplitude,
     sketch,
     out,
+    factor,
     row_pack,
     col_pack,
     row_packs,
@@ -524,7 +525,8 @@
     step = dot(start, gram[...])
     step = dot(step, polynomial[...])
     step = dot(step, polynomial[...])
-    out[...] = (1.5 * start - 0.5 * step) * (math.sqrt(RANK) * lax.rsqrt(scale))
+    out[...] = 1.5 * start - 0.5 * step
+    factor[...] = jnp.broadcast_to(math.sqrt(RANK) * lax.rsqrt(scale), (1, RANK))
 
     drain(len(started))
 
@@ -532,11 +534,14 @@
 def per_device(points, amplitude, sketch):
     f32, bf16 = jnp.float32, jnp.bfloat16
     vmem = pl.BlockSpec(memory_space=pltpu.VMEM)
-    return pl.pallas_call(
+    modes, factor = pl.pallas_call(
         kernel,
-        out_shape=jax.ShapeDtypeStruct((PTS, RANK), f32),
+        out_shape=[
+            jax.ShapeDtypeStruct((PTS, RANK), f32),
+            jax.ShapeDtypeStruct((1, RANK), f32),
+        ],
         in_specs=[vmem] * 3,
-        out_specs=vmem,
+        out_specs=[vmem] * 2,
         scratch_shapes=[
             pltpu.VMEM((8, PTS), f32),
             pltpu.VMEM((8, PTS), f32),
@@ -576,6 +581,7 @@
         ),
         name="kl_modes",
     )(points, amplitude.reshape(1, -1), sketch)
+    return modes * factor
 
 
 def solution(mesh):

time: 77.2 us -> 77.2 us (level)
    unnamed x7 -> x6, local copies, waits for them, and re-layouts: 2.94 us -> 2.24 us
where the time goes in v5:
time: 77.2 us; the launch traced here: 77.1 us
  Pallas kernels  74.1 us (96%)
  local copies, waits for them, and re-layouts  2.24 us (3%)
    pallas_call x1, Pallas kernels, per_device(): pl.pallas_call(kernel, out_shape=[jax.ShapeDtypeStruct((PTS, RANK), f32),...  74.1 us
    unnamed x6, local copies, waits for them, and re-layouts  2.24 us

profile of v5, /device:TPU:1, one launch (start us, length us, event | category | flops | bytes accessed | tf_op | source)
XLA Modules:
  0.0 77.1 jit_solution(1629470237948198110)
XLA Ops:
  0.0 0.0 copy-start.2
  0.0 0.7 copy-done.2
  0.7 0.0 copy-start
  0.7 0.9 %copy-done = bf16[128,512]{1,0:T(8,128)(2,1)S(1)} copy-done((bf16[128,512]{1,0:T(8,128)(2,1)S(1)}, bf16[128,512]{1,0:T(8,128)(2,1)}, u32[]{:S(2)}) %copy-start) | copy-done | bytes 131096
  1.6 0.0 copy-start.1
  1.6 0.7 copy-done.1
  2.2 74.1 %kl_modes.1 = (f32[128,512]{1,0:T(8,128)S(1)}, f32[1,512]{1,0:T(1,128)S(1)}) custom-call(f32[3,128]{1,0:T(4,128)S(1)} %copy-done.1, f32[1,128]{1,0:T(1,128)S(1)} %bitcast.3, bf16[128,512]{1,0:T(8,128)(2,1)S(1)} %copy-done), custom_call_target="tpu_custom_call" | custom-call | flops 7000000000 | bytes 1048576 | tf_op jit(solution)/shard_map/kl_modes/pallas_call | solution.py:537
  76.3 0.7 broadcast_multiply_fusion
Async XLA Ops:
  0.0 0.7 copy-start.2
  0.7 0.9 %copy-start = (bf16[128,512]{1,0:T(8,128)(2,1)S(1)}, bf16[128,512]{1,0:T(8,128)(2,1)}, u32[]{:S(2)}) copy-start(bf16[128,512]{1,0:T(8,128)(2,1)} %sketch.1) | copy-start | bytes 393220
  1.6 0.7 copy-start.1
